TPU v7x, 32 devices: a whole 2x2x4 slice. The times are simulated.
32 devices in a mesh: dp: 8 (over y, x, core), tensor: 4 (over z).
Axes of the slice: x: 2, y: 2, z: 4, core: 2. Of those that a mesh axis runs over, the one named last changes fastest.
Arguments:
- gradients: bfloat16 [8, 8192, 1024], P('dp', 'tensor'), may hold values from -8 to 8
- errors: bfloat16 [8, 8192, 1024], P('dp', 'tensor'), may hold values from -3 to 3
- right_factors: float32 [32, 1024], replicated, may hold values from -6 to 6
Outputs:
- new_errors: bfloat16 [8, 8192, 1024], P('dp', 'tensor')
- new_factors: float32 [32, 1024], replicated
- update: bfloat16 [8192, 1024], P('tensor')
All inputs are finite; a program needn't handle non-finite values.
Results may differ from a plain program's by a relative error of at most 0.001.
Values sent between devices are 32-bit elements; how exact they have to be, the bound alone decides.
A program may use at most 64 MiB of HBM per device.

v0:
```python
import jax
import jax.numpy as jnp
from jax import lax
from jax.sharding import PartitionSpec as P


def per_device(gradients, errors, right_factors):
    highest = lax.Precision.HIGHEST
    replicas = lax.axis_size("dp")
    merged = gradients[0].astype(jnp.float32) + errors[0].astype(jnp.float32)
    local_rows = lax.dot_general(right_factors, merged, (((1,), (1,)), ((), ())), precision=highest)
    p_rows = lax.psum(local_rows, "dp") / replicas
    gram_matrix = lax.psum(jnp.dot(p_rows, p_rows.T, precision=highest), "tensor")
    lower_factor = lax.linalg.cholesky(gram_matrix)
    ortho_rows = lax.linalg.triangular_solve(lower_factor, p_rows, left_side=True, lower=True)
    partial_factors = jnp.dot(ortho_rows, merged, precision=highest)
    within = lax.psum(partial_factors, "tensor")
    new_factors = lax.psum(within, "dp") / replicas
    approx = lax.dot_general(ortho_rows, new_factors, (((0,), (0,)), ((), ())), precision=highest)
    new_errors = (merged - approx).astype(jnp.bfloat16)[None]
    return (new_errors, new_factors, approx.astype(jnp.bfloat16))


def solution(mesh):
    in_specs = (P("dp", "tensor", None), P("dp", "tensor", None), P())
    out_specs = (P("dp", "tensor", None), P(), P("tensor", None))
    return jax.shard_map(
        per_device, mesh=mesh, in_specs=in_specs, out_specs=out_specs, check_vma=False
    )
```

profile of v0, /device:TPU:0, one launch (start us, length us, event | category | flops | bytes accessed | tf_op | source)
XLA Modules:
  0.0 219.5 jit_solution(1397805812250337152)
XLA Ops:
  7.2 0.0 copy-start
  7.2 0.0 all-reduce.4.cloned.1.call-start
  7.2 0.8 copy-done
  8.1 11.6 %fusion.6 = f32[32,2048]{1,0:T(8,128)} fusion(f32[32,1024]{1,0:T(8,128)S(1)} %copy-done, bf16[1,2048,1024]{2,1,0:T(8,128)(2,1)} %param.4, bf16[1,2048,1024]{2,1,0:T(8,128)(2,1)} %param.3), kind=kOutput, calls=%fused_computation.8 | convolution fusion | flops 811597824 | bytes 8781824 | tf_op jit(solution)/shard_map/dot_general | solution.py:11
  19.7 0.0 all-reduce.4.cloned.1.call-update
  19.7 0.0 all-reduce.6.cloned.1.call-start
  19.8 56.3 %all-reduce.4.cloned.1.call-done = f32[32,2048]{1,0:T(8,128)} async-done(((f32[32,2048]{1,0:T(8,128)}), f32[32,2048]{1,0:T(8,128)}) %all-reduce.4.cloned.1.call-update) | async-done | bytes 262160 | tf_op jit(solution)/shard_map/psum | solution.py:12
  76.1 1.4 fusion.11
  77.5 18.7 %psum.29 = f32[32,32]{0,1:T(8,128)S(1)} all-reduce(f32[32,32]{0,1:T(8,128)S(1)} %fusion.11), channel_id=1, replica_groups=mesh['dp'=8,'tensor'=4] {'tensor'}, use_global_device_ids=true, to_apply=%region_1.0 | all-reduce | flops 1024 | bytes 8192 | tf_op jit(solution)/shard_map/psum | solution.py:13
  96.2 0.1 copy.7
  96.3 2.9 %cholesky.16 = f32[32,32]{1,0:T(8,128)S(1)} custom-call(f32[32,32]{1,0:T(8,128)S(1)} %fusion.17), custom_call_target="Cholesky" | custom-call | tf_op jit(solution)/shard_map/cholesky | solution.py:14
  99.3 0.6 compare_reduce_fusion
  99.9 0.7 fusion.15
  100.6 2.4 %custom-call.5 = f32[1,32,32]{1,2,0:T(8,128)S(1)} custom-call(f32[1,32,32]{2,1,0:T(8,128)S(1)} %fusion.15), custom_call_target="InvertDiagBlocksLowerTriangular" | custom-call | tf_op jit(solution)/shard_map/triangular_solve | solution.py:15
  103.0 1.4 fusion.9
  104.4 8.5 %fusion = f32[32,1024]{1,0:T(8,128)} fusion(f32[32,2048]{1,0:T(8,128)S(1)} %fusion.9, bf16[1,2048,1024]{2,1,0:T(8,128)(2,1)} %param.4, bf16[1,2048,1024]{2,1,0:T(8,128)(2,1)} %param.3), kind=kOutput, calls=%fused_computation.1 | convolution fusion | flops 811597824 | bytes 8781824 | tf_op jit(solution)/shard_map/dot_general | solution.py:16
  112.9 0.0 all-reduce.6.cloned.1.call-update
  112.9 0.0 all-reduce.8.cloned.1.call-start
  113.0 31.2 %all-reduce.6.cloned.1.call-done = f32[32,1024]{1,0:T(8,128)} async-done(((f32[32,1024]{1,0:T(8,128)}), f32[32,1024]{1,0:T(8,128)}) %all-reduce.6.cloned.1.call-update) | async-done | bytes 131088 | tf_op jit(solution)/shard_map/psum | solution.py:17
  144.1 0.0 all-reduce.8.cloned.1.call-update
  144.1 55.6 %all-reduce.8.cloned.1.call-done = f32[32,1024]{1,0:T(8,128)} async-done(((f32[32,1024]{1,0:T(8,128)}), f32[32,1024]{1,0:T(8,128)}) %all-reduce.8.cloned.1.call-update) | async-done | bytes 131088 | tf_op jit(solution)/shard_map/psum | solution.py:18
  199.8 0.9 broadcast_multiply_fusion
  200.7 0.0 copy-start.1
  200.7 12.2 %fusion.20 = (bf16[2048,1024]{1,0:T(8,128)(2,1)}, bf16[1,2048,1024]{2,1,0:T(8,128)(2,1)}) fusion(bf16[1,2048,1024]{2,1,0:T(8,128)(2,1)} %param.4, bf16[1,2048,1024]{2,1,0:T(8,128)(2,1)} %param.3, f32[32,2048]{1,0:T(8,128)S(1)} %fusion.9, f32[32,1024]{1,0:T(8,128)S(1)} %broadcast_multiply_fusion), kind=kOutput, calls=%fused_computation.27 | convolution fusion | flops 817889280 | bytes 17170432 | tf_op jit(solution)/shard_map/dot_general | solution.py:19
  212.9 0.0 copy-done.1
  (2 shorter events, 0.0 us)
Async XLA Ops:
  7.2 0.9 copy-start
  7.2 68.9 %all-reduce.4.cloned.1.call-start = ((), (), s32[]{:S(2)}) async-start(), calls=%async_computation | async-start | bytes 524288 | tf_op jit(solution)/shard_map/psum | solution.py:12
  19.7 124.4 %all-reduce.6.cloned.1.call-start = ((), (), s32[]{:S(2)}) async-start(), calls=%async_computation.1 | async-start | bytes 262144 | tf_op jit(solution)/shard_map/psum | solution.py:17
  112.9 86.9 %all-reduce.8.cloned.1.call-start = ((), (), s32[]{:S(2)}) async-start(), calls=%async_computation.2 | async-start | bytes 262144 | tf_op jit(solution)/shard_map/psum | solution.py:18
  200.7 12.2 %copy-start.1 = (f32[32,1024]{1,0:T(8,128)}, f32[32,1024]{1,0:T(8,128)S(1)}, u32[]{:S(2)}) copy-start(f32[32,1024]{1,0:T(8,128)S(1)} %broadcast_multiply_fusion) | copy-start | bytes 393220
Sparse Core Ops, SparseCore 0:
  19.8 56.2 all-reduce.3
  113.0 31.0 all-reduce.5
  147.2 52.5 all-reduce.7
where the time goes:
time: 220 us; the launch traced here: 219 us
  waiting for transfers between devices  143 us (65%)
  matrix products  35.1 us (16%)
  blocking collectives  18.7 us (8%)
  between operations  13.8 us (6%)
  other arithmetic  7.6 us (3%)
    psum x1, waiting for transfers between devices, per_device(): p_rows = lax.psum(local_rows, 'dp') / replicas  56.3 us
    psum x1, waiting for transfers between devices, per_device(): new_factors = lax.psum(within, 'dp') / replicas  55.6 us
    psum x1, waiting for transfers between devices, per_device(): within = lax.psum(partial_factors, 'tensor')  31.2 us
    psum x1, blocking collectives, per_device(): lax.psum(jnp.dot(p_rows, p_rows.T, precision=highest), 'tensor')  18.7 us
    dot_general x1, matrix products, per_device(): lax.dot_general(ortho_rows, new_factors, (((0,), (0,)), ((), ())), precis...  12.2 us
    dot_general x1, matrix products, per_device(): lax.dot_general(right_factors, merged, (((1,), (1,)), ((), ())), precisio...  11.6 us
    dot_general x1, matrix products, per_device(): partial_factors = jnp.dot(ortho_rows, merged, precision=highest)  8.49 us
  transfers between devices with their start and end apart: 3, of which 3 were waited for; matrix products, arithmetic and copies ran while one was open for 0% of the time, Pallas kernels for 0%

commit v1 on v0

v1 whole, which is shorter than its diff:
```python
import functools

import jax
import jax.numpy as jnp
from jax import lax
from jax.experimental import pallas as pl
from jax.experimental.pallas import tpu as pltpu
from jax.sharding import PartitionSpec as P

MESH = pl.DeviceIdType.MESH
F32 = jnp.float32
BF16 = jnp.bfloat16
HIGHEST = lax.Precision.HIGHEST


def split3(x):
    hi = x.astype(BF16)
    rest = x - hi.astype(F32)
    mid = rest.astype(BF16)
    low = (rest - mid.astype(F32)).astype(BF16)
    return hi, mid, low


def inverse_factor(gram, rank):
    rows = lax.broadcasted_iota(jnp.int32, (rank, 128), 0)
    lanes = lax.broadcasted_iota(jnp.int32, (rank, 128), 1)
    both = jnp.where(lanes == rows + rank, 1.0, gram)
    scale = jnp.ones((rank, 128), F32)
    for k in range(rank):
        column = jnp.broadcast_to(both[:, k : k + 1], (rank, 128))
        pivot = column[k : k + 1, :]
        scale = jnp.where(rows == k, pivot, scale)
        factor = jnp.where(rows > k, column * (1.0 / pivot), 0.0)
        both = both - factor * both[k : k + 1, :]
    both = both / jnp.sqrt(scale)
    return both[:, rank : 2 * rank]


def reduce_kernel(
    n_dp, n_t, own_p, own_s,
    g_hbm, e_hbm, r_hbm, ortho_ref, q_ref,
    g_v, e_v, r_v, p_loc, p_in, p_full, s_acc, s_loc, s_in, z_in, q_full,
    gram_k, gram_in,
    g_sem, e_sem, r_sem,
    ps_send, ps_recv, pg_send, pg_recv, gr_send, gr_recv,
    ss_send, ss_recv, z_send, z_recv, q_send, q_recv,
):
    me = lax.axis_index("dp")
    mt = lax.axis_index("tensor")
    rank = r_v.shape[0]
    width = g_v.shape[1]
    cols = s_loc.shape[2]

    def peer(k):
        return lax.rem(me + k, n_dp)

    def tpeer(k):
        return lax.rem(mt + k, n_t)

    def chunk(d):
        return lax.rem(me + d, own_p)

    def remote(src, dst, send, recv, dp, t):
        return pltpu.make_async_remote_copy(
            src_ref=src, dst_ref=dst, send_sem=send, recv_sem=recv,
            device_id=(dp, t), device_id_type=MESH,
        )

    def guard(condition, always):
        if always:
            return lambda f: f()
        return pl.when(condition)

    def load(c):
        return (
            pltpu.make_async_copy(g_hbm.at[0, pl.ds(c * width, width)], g_v.at[c], g_sem.at[c]),
            pltpu.make_async_copy(e_hbm.at[0, pl.ds(c * width, width)], e_v.at[c], e_sem.at[c]),
        )

    r_copy = pltpu.make_async_copy(r_hbm, r_v, r_sem)
    r_copy.start()
    for d in range(1, own_p + 1):
        for copy in load(chunk(d)):
            copy.start()

    gram_k[...] = jnp.zeros_like(gram_k)
    barrier = pltpu.get_barrier_semaphore()
    for k in range(1, n_dp):
        pl.semaphore_signal(barrier, inc=1, device_id=(peer(k), mt), device_id_type=MESH)
    for k in range(1, n_t):
        pl.semaphore_signal(barrier, inc=1, device_id=(me, tpeer(k)), device_id_type=MESH)

    r_copy.wait()
    r3 = jnp.concatenate(split3(r_v[...]), axis=0)
    pl.semaphore_wait(barrier, n_dp - 1 + n_t - 1)

    def fold(x):
        return x[:rank] + x[rank : 2 * rank] + x[2 * rank :]

    nt = (((1,), (1,)), ((), ()))

    for d in range(1, own_p + 1):
        c = chunk(d)
        for copy in load(c):
            copy.wait()
        both = lax.dot_general(r3, g_v[c], nt, preferred_element_type=F32)
        both += lax.dot_general(r3, e_v[c], nt, preferred_element_type=F32)
        p_loc[c] = fold(both)
        if not (own_p == n_dp and d == own_p):
            @guard(c != me, own_p == n_dp)
            def _():
                remote(p_loc.at[c], p_in.at[me], ps_send.at[c], ps_recv.at[me], c, mt).start()

    is_p = me < own_p

    @guard(is_p, own_p == n_dp)
    def _():
        total = p_loc[me]
        for k in range(1, n_dp):
            o = peer(k)
            remote(p_loc.at[0], p_in.at[o], ps_send.at[0], ps_recv.at[o], o, mt).wait_recv()
            total = total + p_in[o]
        p_full[me] = total / n_dp
        for k in range(1, n_dp):
            o = peer(k)
            remote(p_full.at[me], p_full.at[me], pg_send.at[o], pg_recv.at[me], o, mt).start()

    for d in range(own_p):
        c = chunk(d)
        if not (own_p == n_dp and d == 0):
            @guard(c != me, own_p == n_dp)
            def _():
                remote(p_full.at[c], p_full.at[c], pg_send.at[0], pg_recv.at[c], c, mt).wait_recv()
        p = p_full[c]
        gram_k[c, :, :rank] = lax.dot_general(p, p, nt, precision=HIGHEST, preferred_element_type=F32)
        if d == own_p - 1:
            gram = gram_k[0]
            for k in range(1, own_p):
                gram = gram + gram_k[k]
            gram_in[mt] = gram
            for k in range(1, n_t):
                o = tpeer(k)
                remote(gram_in.at[mt], gram_in.at[mt], gr_send.at[o], gr_recv.at[mt], me, o).start()
        p3 = jnp.concatenate(split3(p), axis=0)
        both = jnp.dot(p3, g_v[c], preferred_element_type=F32)
        both += jnp.dot(p3, e_v[c], preferred_element_type=F32)
        if d == 0:
            s_acc[...] = fold(both)
        else:
            s_acc[...] += fold(both)

    for j in range(own_s):
        s_loc[j] = s_acc[:, j * cols : (j + 1) * cols]
    for d in range(1, own_s + 1):
        j = lax.rem(me + d, own_s)
        if not (own_s == n_dp and d == own_s):
            @guard(j != me, own_s == n_dp)
            def _():
                remote(s_loc.at[j], s_in.at[me], ss_send.at[j], ss_recv.at[me], j, mt).start()

    for k in range(1, n_t):
        o = tpeer(k)
        remote(gram_in.at[o], gram_in.at[o], gr_send.at[0], gr_recv.at[o], me, o).wait_recv()
    gram = gram_in[0]
    for k in range(1, n_t):
        gram = gram + gram_in[k]
    lanes = lax.broadcasted_iota(jnp.int32, (rank, 128), 1)
    gram = jnp.where(lanes < rank, gram, 0.0)
    is_s = me < own_s

    def share_sum():
        total = s_loc[me]
        for k in range(1, n_dp):
            o = peer(k)
            remote(s_loc.at[0], s_in.at[o], ss_send.at[0], ss_recv.at[o], o, mt).wait_recv()
            total = total + s_in[o]
        z_in[mt] = total
        for k in range(1, n_t):
            o = tpeer(k)
            remote(z_in.at[mt], z_in.at[mt], z_send.at[o], z_recv.at[mt], me, o).start()

    guard(is_s, own_s == n_dp)(share_sum)
    inverse = inverse_factor(gram, rank)

    @guard(is_s, own_s == n_dp)
    def _():
        for k in range(1, n_t):
            o = tpeer(k)
            remote(z_in.at[o], z_in.at[o], z_send.at[0], z_recv.at[o], me, o).wait_recv()
        total = z_in[0]
        for k in range(1, n_t):
            total = total + z_in[k]
        q_full[me] = jnp.dot(inverse, total / n_dp, precision=HIGHEST, preferred_element_type=F32)
        for k in range(1, n_dp):
            o = peer(k)
            remote(q_full.at[me], q_full.at[me], q_send.at[o], q_recv.at[me], o, mt).start()

    for c in range(own_p):
        ortho_ref[:, c * width : (c + 1) * width] = jnp.dot(
            inverse, p_full[c], precision=HIGHEST, preferred_element_type=F32
        )

    for d in range(1, own_s + 1):
        j = lax.rem(me + d, own_s)
        if not (own_s == n_dp and d == own_s):
            @guard(j != me, own_s == n_dp)
            def _():
                remote(q_full.at[j], q_full.at[j], q_send.at[0], q_recv.at[j], j, mt).wait_recv()
    for j in range(own_s):
        q_ref[:, j * cols : (j + 1) * cols] = q_full[j]

    for d in range(1, own_p + 1):
        c = chunk(d)
        if not (own_p == n_dp and d == own_p):
            @guard(c != me, own_p == n_dp)
            def _():
                remote(p_loc.at[c], p_in.at[me], ps_send.at[c], ps_recv.at[me], c, mt).wait_send()
    for d in range(1, own_s + 1):
        j = lax.rem(me + d, own_s)
        if not (own_s == n_dp and d == own_s):
            @guard(j != me, own_s == n_dp)
            def _():
                remote(s_loc.at[j], s_in.at[me], ss_send.at[j], ss_recv.at[me], j, mt).wait_send()
    for k in range(1, n_t):
        o = tpeer(k)
        remote(gram_in.at[mt], gram_in.at[mt], gr_send.at[o], gr_recv.at[mt], me, o).wait_send()

    @guard(is_p, own_p == n_dp)
    def _():
        for k in range(1, n_dp):
            o = peer(k)
            remote(p_full.at[me], p_full.at[me], pg_send.at[o], pg_recv.at[me], o, mt).wait_send()

    @guard(is_s, own_s == n_dp)
    def _():
        for k in range(1, n_dp):
            o = peer(k)
            remote(q_full.at[me], q_full.at[me], q_send.at[o], q_recv.at[me], o, mt).wait_send()
        for k in range(1, n_t):
            o = tpeer(k)
            remote(z_in.at[mt], z_in.at[mt], z_send.at[o], z_recv.at[mt], me, o).wait_send()


def apply_kernel(g_ref, e_ref, ortho_ref, q_ref, err_ref, factors_ref, update_ref, q6_ref):
    @pl.when(pl.program_id(0) == 0)
    def _():
        q = q_ref[...]
        factors_ref[...] = q
        hi, mid, low = split3(q)
        q6_ref[...] = jnp.concatenate([hi, mid, hi, low, mid, hi], axis=0)

    hi, mid, low = split3(ortho_ref[...])
    left = jnp.concatenate([hi, hi, mid, hi, mid, low], axis=0)
    approx = lax.dot_general(
        left, q6_ref[...], (((0,), (0,)), ((), ())), preferred_element_type=F32
    )
    update_ref[...] = approx.astype(BF16)
    err_ref[0] = ((g_ref[0].astype(F32) + e_ref[0].astype(F32)) - approx).astype(BF16)


def per_device(gradients, errors, right_factors):
    n_dp, n_t = lax.axis_size("dp"), lax.axis_size("tensor")
    rows, kv = gradients.shape[1:]
    rank = right_factors.shape[0]
    own_p = min(n_dp, rows // 128)
    own_s = min(n_dp, kv // 128)
    width, cols = rows // own_p, kv // own_s
    dma = pltpu.SemaphoreType.DMA
    ortho, q = pl.pallas_call(
        functools.partial(reduce_kernel, n_dp, n_t, own_p, own_s),
        out_shape=(
            jax.ShapeDtypeStruct((rank, rows), F32),
            jax.ShapeDtypeStruct((rank, kv), F32),
        ),
        in_specs=[pl.BlockSpec(memory_space=pl.ANY)] * 3,
        out_specs=(pl.BlockSpec(memory_space=pltpu.VMEM),) * 2,
        scratch_shapes=[
            pltpu.VMEM((own_p, width, kv), BF16),
            pltpu.VMEM((own_p, width, kv), BF16),
            pltpu.VMEM((rank, kv), F32),
            pltpu.VMEM((own_p, rank, width), F32),
            pltpu.VMEM((n_dp, rank, width), F32),
            pltpu.VMEM((own_p, rank, width), F32),
            pltpu.VMEM((rank, kv), F32),
            pltpu.VMEM((own_s, rank, cols), F32),
            pltpu.VMEM((n_dp, rank, cols), F32),
            pltpu.VMEM((n_t, rank, cols), F32),
            pltpu.VMEM((own_s, rank, cols), F32),
            pltpu.VMEM((own_p, rank, 128), F32),
            pltpu.VMEM((n_t, rank, 128), F32),
            dma((own_p,)), dma((own_p,)), dma,
            dma((own_p,)), dma((n_dp,)), dma((n_dp,)), dma((own_p,)),
            dma((n_t,)), dma((n_t,)),
            dma((own_s,)), dma((n_dp,)), dma((n_t,)), dma((n_t,)),
            dma((n_dp,)), dma((own_s,)),
        ],
        compiler_params=pltpu.CompilerParams(
            collective_id=0, has_side_effects=True, vmem_limit_bytes=40 * 2**20
        ),
    )(gradients, errors, right_factors)

    block = min(256, rows)
    big = pl.BlockSpec((1, block, kv), lambda i: (0, i, 0))
    return pl.pallas_call(
        apply_kernel,
        grid=(rows // block,),
        out_shape=(
            jax.ShapeDtypeStruct((1, rows, kv), BF16),
            jax.ShapeDtypeStruct((rank, kv), F32),
            jax.ShapeDtypeStruct((rows, kv), BF16),
        ),
        in_specs=[
            big, big,
            pl.BlockSpec((rank, block), lambda i: (0, i)),
            pl.BlockSpec((rank, kv), lambda i: (0, 0)),
        ],
        out_specs=(
            big,
            pl.BlockSpec((rank, kv), lambda i: (0, 0)),
            pl.BlockSpec((block, kv), lambda i: (i, 0)),
        ),
        scratch_shapes=[pltpu.VMEM((6 * rank, kv), BF16)],
        compiler_params=pltpu.CompilerParams(vmem_limit_bytes=40 * 2**20),
    )(gradients, errors, ortho, q)


def solution(mesh):
    in_specs = (P("dp", "tensor", None), P("dp", "tensor", None), P())
    out_specs = (P("dp", "tensor", None), P(), P("tensor", None))
    return jax.shard_map(
        per_device, mesh=mesh, in_specs=in_specs, out_specs=out_specs, check_vma=False
    )
```

time: 220 us -> 47.1 us (0.21)
  waiting for transfers between devices: 143 us -> 0 us
  Pallas kernels: 0 us -> 41 us
  matrix products: 35.1 us -> 0 us
  blocking collectives: 18.7 us -> 0 us
  between operations: 13.8 us -> 0.65 us
  other arithmetic: 7.6 us -> 0 us
  local copies, waits for them, and re-layouts: 0.94 us -> 5.27 us
    psum x3 -> x0, waiting for transfers between devices: 143 us -> none  [the longest x1 56.3 us: per_device(): p_rows = lax.psum(local_rows, 'dp') / replicas]
    pallas_call x0 -> x2, Pallas kernels: none -> 41 us  [the longest x1 35.4 us: per_device(): pl.pallas_call(functools.partial(reduce_kernel, n_dp, n_t, own_p, own_s),...]
    dot_general x4 -> x0, matrix products: 33.7 us -> none  [the longest x1 12.2 us: per_device(): lax.dot_general(ortho_rows, new_factors, (((0,), (0,)), ((), ())), precis...]
    psum x1 -> x0, blocking collectives: 18.7 us -> none  [per_device(): lax.psum(jnp.dot(p_rows, p_rows.T, precision=highest), 'tensor')]
    another operation x5 -> x0, other arithmetic: 6.68 us -> none  [the longest x3 3.59 us: per_device(): lower_factor = lax.linalg.cholesky(gram_matrix)]
    unnamed x4 -> x6, local copies, waits for them, and re-layouts: 0.86 us -> 5.27 us
  transfers between devices with their start and end apart: 3 -> 0, of which waited for: 3 -> 0; matrix products, arithmetic and copies ran while one was open for 0% -> 0% of each run, Pallas kernels for 0% -> 0%
where the time goes in v1:
time: 47.1 us; the launch traced here: 46.9 us
  Pallas kernels  41 us (87%)
  local copies, waits for them, and re-layouts  5.27 us (11%)
  between operations  0.65 us (1%)
    pallas_call x1, Pallas kernels, per_device(): pl.pallas_call(functools.partial(reduce_kernel, n_dp, n_t, own_p, own_s),...  35.4 us
    pallas_call x1, Pallas kernels, per_device(): pl.pallas_call(apply_kernel, grid=(rows // block,), out_shape=(jax.ShapeD...  5.56 us
    unnamed x6, local copies, waits for them, and re-layouts  5.27 us

profile of v1, /device:TPU:0, one launch (start us, length us, event | category | flops | bytes accessed | tf_op | source)
XLA Modules:
  0.0 46.9 jit_solution(12977219163920845028)
XLA Ops:
  0.6 0.0 copy-start
  0.6 2.2 %copy-done = bf16[1,2048,1024]{2,1,0:T(8,128)(2,1)S(1)} copy-done((bf16[1,2048,1024]{2,1,0:T(8,128)(2,1)S(1)}, bf16[1,2048,1024]{2,1,0:T(8,128)(2,1)}, u32[]{:S(2)}) %copy-start) | copy-done | bytes 4194328
  2.8 0.0 copy-start.1
  2.8 2.2 %copy-done.1 = bf16[1,2048,1024]{2,1,0:T(8,128)(2,1)S(1)} copy-done((bf16[1,2048,1024]{2,1,0:T(8,128)(2,1)S(1)}, bf16[1,2048,1024]{2,1,0:T(8,128)(2,1)}, u32[]{:S(2)}) %copy-start.1) | copy-done | bytes 4194328
  5.0 0.0 copy-start.2
  5.0 0.9 %copy-done.2 = f32[32,1024]{1,0:T(8,128)S(1)} copy-done((f32[32,1024]{1,0:T(8,128)S(1)}, f32[32,1024]{1,0:T(8,128)}, u32[]{:S(2)}) %copy-start.2) | copy-done | bytes 131096
  5.9 35.4 %shard_map.58 = (f32[32,2048]{1,0:T(8,128)S(1)}, f32[32,1024]{1,0:T(8,128)S(1)}) custom-call(bf16[1,2048,1024]{2,1,0:T(8,128)(2,1)S(1)} %copy-done, bf16[1,2048,1024]{2,1,0:T(8,128)(2,1)S(1)} %copy-done.1, f32[32,1024]{1,0:T(8,128)S(1)} %copy-done.2), custom_call_target="tpu_custom_call" | custom-call | tf_op jit(solution)/shard_map/pallas_call | solution.py:269
  41.3 5.6 %shard_map.59 = (bf16[1,2048,1024]{2,1,0:T(8,128)(2,1)}, f32[32,1024]{1,0:T(8,128)}, bf16[2048,1024]{1,0:T(8,128)(2,1)}) custom-call(bf16[1,2048,1024]{2,1,0:T(8,128)(2,1)S(1)} %copy-done, bf16[1,2048,1024]{2,1,0:T(8,128)(2,1)S(1)} %copy-done.1, f32[32,2048]{1,0:T(8,128)S(1)} %get-tuple-element.5.ortho_ref, f32[32,1024]{1,0:T(8,128)S(1)} %get-tuple-element.6.q_ref), custom_call_target="tpu_custom_call" | custom-call | tf_op jit(solution)/shard_map/pallas_call | solution.py:304
Async XLA Ops:
  0.6 2.2 %copy-start = (bf16[1,2048,1024]{2,1,0:T(8,128)(2,1)S(1)}, bf16[1,2048,1024]{2,1,0:T(8,128)(2,1)}, u32[]{:S(2)}) copy-start(bf16[1,2048,1024]{2,1,0:T(8,128)(2,1)} %g_ref.1) | copy-start | bytes 12582916
  2.8 2.2 %copy-start.1 = (bf16[1,2048,1024]{2,1,0:T(8,128)(2,1)S(1)}, bf16[1,2048,1024]{2,1,0:T(8,128)(2,1)}, u32[]{:S(2)}) copy-start(bf16[1,2048,1024]{2,1,0:T(8,128)(2,1)} %e_ref.1) | copy-start | bytes 12582916
  5.0 0.9 %copy-start.2 = (f32[32,1024]{1,0:T(8,128)S(1)}, f32[32,1024]{1,0:T(8,128)}, u32[]{:S(2)}) copy-start(f32[32,1024]{1,0:T(8,128)} %r_hbm.1) | copy-start | bytes 393220

commit v2 on v1

--- a/solution.py
+++ b/solution.py
@@ -21,25 +21,22 @@
     return hi, mid, low
 
 
-def inverse_factor(gram, rank):
+def eliminate(both, scale, first, last):
+    rank = both.shape[0]
     rows = lax.broadcasted_iota(jnp.int32, (rank, 128), 0)
-    lanes = lax.broadcasted_iota(jnp.int32, (rank, 128), 1)
-    both = jnp.where(lanes == rows + rank, 1.0, gram)
-    scale = jnp.ones((rank, 128), F32)
-    for k in range(rank):
+    for k in range(first, last):
         column = jnp.broadcast_to(both[:, k : k + 1], (rank, 128))
         pivot = column[k : k + 1, :]
         scale = jnp.where(rows == k, pivot, scale)
         factor = jnp.where(rows > k, column * (1.0 / pivot), 0.0)
         both = both - factor * both[k : k + 1, :]
-    both = both / jnp.sqrt(scale)
-    return both[:, rank : 2 * rank]
+    return both, scale
 
 
 def reduce_kernel(
     n_dp, n_t, own_p, own_s,
-    g_hbm, e_hbm, r_hbm, ortho_ref, q_ref,
-    g_v, e_v, r_v, p_loc, p_in, p_full, s_acc, s_loc, s_in, z_in, q_full,
+    g_hbm, e_hbm, r_hbm, g_v, e_v, ortho_ref, q_ref,
+    r_v, p_loc, p_in, p_full, s_acc, s_loc, s_in, z_in, q_full,
     gram_k, gram_in,
     g_sem, e_sem, r_sem,
     ps_send, ps_recv, pg_send, pg_recv, gr_send, gr_recv,
@@ -92,7 +89,6 @@
 
     r_copy.wait()
     r3 = jnp.concatenate(split3(r_v[...]), axis=0)
-    pl.semaphore_wait(barrier, n_dp - 1 + n_t - 1)
 
     def fold(x):
         return x[:rank] + x[rank : 2 * rank] + x[2 * rank :]
@@ -106,6 +102,8 @@
         both = lax.dot_general(r3, g_v[c], nt, preferred_element_type=F32)
         both += lax.dot_general(r3, e_v[c], nt, preferred_element_type=F32)
         p_loc[c] = fold(both)
+        if d == 1:
+            pl.semaphore_wait(barrier, n_dp - 1 + n_t - 1)
         if not (own_p == n_dp and d == own_p):
             @guard(c != me, own_p == n_dp)
             def _():
@@ -165,7 +163,11 @@
     for k in range(1, n_t):
         gram = gram + gram_in[k]
     lanes = lax.broadcasted_iota(jnp.int32, (rank, 128), 1)
+    rows = lax.broadcasted_iota(jnp.int32, (rank, 128), 0)
     gram = jnp.where(lanes < rank, gram, 0.0)
+    both = jnp.where(lanes == rows + rank, 1.0, gram)
+    scale = jnp.ones((rank, 128), F32)
+    half = rank // 2
     is_s = me < own_s
 
     def share_sum():
@@ -180,7 +182,7 @@
             remote(z_in.at[mt], z_in.at[mt], z_send.at[o], z_recv.at[mt], me, o).start()
 
     guard(is_s, own_s == n_dp)(share_sum)
-    inverse = inverse_factor(gram, rank)
+    both, scale = eliminate(both, scale, 0, half)
 
     @guard(is_s, own_s == n_dp)
     def _():
@@ -190,11 +192,13 @@
         total = z_in[0]
         for k in range(1, n_t):
             total = total + z_in[k]
-        q_full[me] = jnp.dot(inverse, total / n_dp, precision=HIGHEST, preferred_element_type=F32)
+        q_full[me] = total / n_dp
         for k in range(1, n_dp):
             o = peer(k)
             remote(q_full.at[me], q_full.at[me], q_send.at[o], q_recv.at[me], o, mt).start()
 
+    both, scale = eliminate(both, scale, half, rank)
+    inverse = (both / jnp.sqrt(scale))[:, rank : 2 * rank]
     for c in range(own_p):
         ortho_ref[:, c * width : (c + 1) * width] = jnp.dot(
             inverse, p_full[c], precision=HIGHEST, preferred_element_type=F32
@@ -207,7 +211,9 @@
             def _():
                 remote(q_full.at[j], q_full.at[j], q_send.at[0], q_recv.at[j], j, mt).wait_recv()
     for j in range(own_s):
-        q_ref[:, j * cols : (j + 1) * cols] = q_full[j]
+        q_ref[:, j * cols : (j + 1) * cols] = jnp.dot(
+            inverse, q_full[j], precision=HIGHEST, preferred_element_type=F32
+        )
 
     for d in range(1, own_p + 1):
         c = chunk(d)
@@ -266,17 +272,17 @@
     own_s = min(n_dp, kv // 128)
     width, cols = rows // own_p, kv // own_s
     dma = pltpu.SemaphoreType.DMA
-    ortho, q = pl.pallas_call(
+    held_g, held_e, ortho, q = pl.pallas_call(
         functools.partial(reduce_kernel, n_dp, n_t, own_p, own_s),
         out_shape=(
-            jax.ShapeDtypeStruct((rank, rows), F32),
-            jax.ShapeDtypeStruct((rank, kv), F32),
+            pltpu.VMEM((own_p, width, kv), BF16),
+            pltpu.VMEM((own_p, width, kv), BF16),
+            pltpu.VMEM((rank, rows), F32),
+            pltpu.VMEM((rank, kv), F32),
         ),
         in_specs=[pl.BlockSpec(memory_space=pl.ANY)] * 3,
-        out_specs=(pl.BlockSpec(memory_space=pltpu.VMEM),) * 2,
+        out_specs=(pl.BlockSpec(memory_space=pltpu.VMEM),) * 4,
         scratch_shapes=[
-            pltpu.VMEM((own_p, width, kv), BF16),
-            pltpu.VMEM((own_p, width, kv), BF16),
             pltpu.VMEM((rank, kv), F32),
             pltpu.VMEM((own_p, rank, width), F32),
             pltpu.VMEM((n_dp, rank, width), F32),
@@ -295,11 +301,12 @@
             dma((n_dp,)), dma((own_s,)),
         ],
         compiler_params=pltpu.CompilerParams(
-            collective_id=0, has_side_effects=True, vmem_limit_bytes=40 * 2**20
+            collective_id=0, has_side_effects=True, vmem_limit_bytes=51 * 2**20
         ),
     )(gradients, errors, right_factors)
 
-    block = min(256, rows)
+    block = width
+    held = pl.BlockSpec((1, block, kv), lambda i: (i, 0, 0))
     big = pl.BlockSpec((1, block, kv), lambda i: (0, i, 0))
     return pl.pallas_call(
         apply_kernel,
@@ -310,7 +317,7 @@
             jax.ShapeDtypeStruct((rows, kv), BF16),
         ),
         in_specs=[
-            big, big,
+            held, held,
             pl.BlockSpec((rank, block), lambda i: (0, i)),
             pl.BlockSpec((rank, kv), lambda i: (0, 0)),
         ],
@@ -321,7 +328,7 @@
         ),
         scratch_shapes=[pltpu.VMEM((6 * rank, kv), BF16)],
         compiler_params=pltpu.CompilerParams(vmem_limit_bytes=40 * 2**20),
-    )(gradients, errors, ortho, q)
+    )(held_g, held_e, ortho, q)
 
 
 def solution(mesh):

time: 47.1 us -> 40.4 us (0.86)
  local copies, waits for them, and re-layouts: 5.27 us -> 0 us
  Pallas kernels: 41 us -> 39.6 us
    unnamed x6 -> x0, local copies, waits for them, and re-layouts: 5.27 us -> none
    pallas_call x1, Pallas kernels: 35.4 us -> 34.1 us  [per_device(): pl.pallas_call(functools.partial(reduce_kernel, n_dp, n_t, own_p, own_s),...]
where the time goes in v2:
time: 40.4 us; the launch traced here: 40.3 us
  Pallas kernels  39.6 us (98%)
  between operations  0.64 us (2%)
    pallas_call x1, Pallas kernels, per_device(): pl.pallas_call(functools.partial(reduce_kernel, n_dp, n_t, own_p, own_s),...  34.1 us
    pallas_call x1, Pallas kernels, per_device(): pl.pallas_call(apply_kernel, grid=(rows // block,), out_shape=(jax.ShapeD...  5.56 us

profile of v2, /device:TPU:0, one launch (start us, length us, event | category | flops | bytes accessed | tf_op | source)
XLA Modules:
  0.0 40.3 jit_solution(11566107965636783683)
XLA Ops:
  0.6 34.1 %shard_map.58 = (bf16[8,256,1024]{2,1,0:T(8,128)(2,1)S(1)}, bf16[8,256,1024]{2,1,0:T(8,128)(2,1)S(1)}, f32[32,2048]{1,0:T(8,128)S(1)}, f32[32,1024]{1,0:T(8,128)S(1)}) custom-call(bf16[1,2048,1024]{2,1,0:T(8,128)(2,1)} %g_hbm.1, bf16[1,2048,1024]{2,1,0:T(8,128)(2,1)} %e_hbm.1, f32[32,1024]{1,0:T(8,128)} %r_hbm.1), custom_call_target="tpu_custom_call" | custom-call | tf_op jit(solution)/shard_map/pallas_call | solution.py:275
  34.7 5.6 %shard_map.59 = (bf16[1,2048,1024]{2,1,0:T(8,128)(2,1)}, f32[32,1024]{1,0:T(8,128)}, bf16[2048,1024]{1,0:T(8,128)(2,1)}) custom-call(bf16[8,256,1024]{2,1,0:T(8,128)(2,1)S(1)} %get-tuple-element.7.g_ref, bf16[8,256,1024]{2,1,0:T(8,128)(2,1)S(1)} %get-tuple-element.8.e_ref, f32[32,2048]{1,0:T(8,128)S(1)} %get-tuple-element.9.ortho_ref, ...), custom_call_target="tpu_custom_call" | custom-call | tf_op jit(solution)/shard_map/pallas_call | solution.py:311

commit v3 on v2

--- a/solution.py
+++ b/solution.py
@@ -261,7 +261,8 @@
         left, q6_ref[...], (((0,), (0,)), ((), ())), preferred_element_type=F32
     )
     update_ref[...] = approx.astype(BF16)
-    err_ref[0] = ((g_ref[0].astype(F32) + e_ref[0].astype(F32)) - approx).astype(BF16)
+    merged = g_ref[...].astype(F32) + e_ref[...].astype(F32)
+    err_ref[0] = (merged.reshape(approx.shape) - approx).astype(BF16)
 
 
 def per_device(gradients, errors, right_factors):
@@ -305,8 +306,9 @@
         ),
     )(gradients, errors, right_factors)
 
-    block = width
-    held = pl.BlockSpec((1, block, kv), lambda i: (i, 0, 0))
+    per = 2 if own_p % 2 == 0 else 1
+    block = per * width
+    held = pl.BlockSpec((per, width, kv), lambda i: (i, 0, 0))
     big = pl.BlockSpec((1, block, kv), lambda i: (0, i, 0))
     return pl.pallas_call(
         apply_kernel,

time: 40.4 us -> 39.2 us (0.970)
  Pallas kernels: 39.6 us -> 38.4 us
    pallas_call x1, Pallas kernels: 5.56 us -> 4.36 us  [per_device(): pl.pallas_call(apply_kernel, grid=(rows // block,), out_shape=(jax.ShapeD...]
where the time goes in v3:
time: 39.2 us; the launch traced here: 39.1 us
  Pallas kernels  38.4 us (98%)
  between operations  0.64 us (2%)
    pallas_call x1, Pallas kernels, per_device(): pl.pallas_call(functools.partial(reduce_kernel, n_dp, n_t, own_p, own_s),...  34.1 us
    pallas_call x1, Pallas kernels, per_device(): pl.pallas_call(apply_kernel, grid=(rows // block,), out_shape=(jax.ShapeD...  4.36 us

profile of v3, /device:TPU:0, one launch (start us, length us, event | category | flops | bytes accessed | tf_op | source)
XLA Modules:
  0.0 39.1 jit_solution(13742148156381354947)
XLA Ops:
  0.6 34.1 %shard_map.58 = (bf16[8,256,1024]{2,1,0:T(8,128)(2,1)S(1)}, bf16[8,256,1024]{2,1,0:T(8,128)(2,1)S(1)}, f32[32,2048]{1,0:T(8,128)S(1)}, f32[32,1024]{1,0:T(8,128)S(1)}) custom-call(bf16[1,2048,1024]{2,1,0:T(8,128)(2,1)} %g_hbm.1, bf16[1,2048,1024]{2,1,0:T(8,128)(2,1)} %e_hbm.1, f32[32,1024]{1,0:T(8,128)} %r_hbm.1), custom_call_target="tpu_custom_call" | custom-call | tf_op jit(solution)/shard_map/pallas_call | solution.py:276
  34.7 4.4 %shard_map.59 = (bf16[1,2048,1024]{2,1,0:T(8,128)(2,1)}, f32[32,1024]{1,0:T(8,128)}, bf16[2048,1024]{1,0:T(8,128)(2,1)}) custom-call(bf16[8,256,1024]{2,1,0:T(8,128)(2,1)S(1)} %get-tuple-element.7.g_ref, bf16[8,256,1024]{2,1,0:T(8,128)(2,1)S(1)} %get-tuple-element.8.e_ref, f32[32,2048]{1,0:T(8,128)S(1)} %get-tuple-element.9.ortho_ref, ...), custom_call_target="tpu_custom_call" | custom-call | tf_op jit(solution)/shard_map/pallas_call | solution.py:313
